TPU v7x, 512 devices: a whole 4x4x16 slice. The times are simulated.
512 devices in a mesh: dp: 32 (over x, y, core), seq: 16 (over z).
Axes of the slice: x: 4, y: 4, z: 16, core: 2. Of those that a mesh axis runs over, the one named last changes fastest.
Arguments:
- tile_tokens: bfloat16 [32, 512, 3200], P('dp', 'seq'), may hold values from -6 to 6
- proj_weight: bfloat16 [3200, 8192], P('dp', 'seq')
- text_hidden: bfloat16 [32, 2048, 8192], P('dp', 'seq'), may hold values from -6 to 6
- cotangent: bfloat16 [32, 2048, 8192], P('dp', 'seq'), may hold values from -1.1953125 to 1.1953125
- norm_gain: float32 [8192], replicated, may hold values from 0.25 to 1.75
- placeholders: int32 [32, 512], P('dp'), may hold values from 0 to 2047, as said below
- bucket_levels: int32 [32, 16, 3200], P('dp', 'seq'), may hold values from 2 to 16
- row_draws: float32 [32, 16, 3200], P('dp', 'seq'), may hold values from 0 to 1
- column_draws: float32 [32, 8192], P('dp', 'seq'), may hold values from 0 to 1
Outputs:
- weight_grad: float32 [3200, 8192], P('dp', 'seq')
- gain_grad: float32 [8192], replicated
Inputs may be any that keep to these rules, and one draw needn't show every extreme that they name: Each row is strictly increasing. Among the positions of one device's block of 128 positions stand at most 48 placeholders, and in every row some block holds exactly 48.
All inputs are finite; a program needn't handle non-finite values.
Results may differ from a plain program's by a relative error of at most 0.014.
Values may be sent and summed in bfloat16 or wider, within the bound.
A program may use at most 64 MiB of HBM per device.

v0:
```python
import jax
import jax.numpy as jnp
from jax import lax
from jax.sharding import Mesh
from jax.sharding import PartitionSpec as P

IMG_MOST = 48
DP = ("dp_0", "dp_1", "dp_2")
DP_SEQ = ("dp_0", "dp_1", "dp_2", "seq")
EPSILON = 1e-06


def copy_for_each(value, axis):
    copies = jnp.broadcast_to(value, (lax.axis_size(axis), *value.shape))
    return lax.all_to_all(copies, axis, split_axis=0, concat_axis=0, tiled=True)


def of_everyone(value, axis):
    everything = copy_for_each(value, axis)
    return jnp.sum(everything, axis=0)


def in_one(arrays, axis):
    ravelled, at, outs = (jnp.concatenate([a.reshape(-1) for a in arrays]), 0, [])
    so_far = of_everyone(ravelled, axis)
    for a in arrays:
        outs.append(so_far[at : at + a.size].reshape(a.shape))
        at += a.size
    return tuple(outs)


def one_axis_at_a_time(value, axes):
    for axis in axes:
        value = lax.psum(value, axis)
    return value


def quantize(gradient, levels_now, rows_now, columns_now):
    bucket_norm = jnp.sqrt(jnp.sum(gradient * gradient, axis=1, keepdims=True) + EPSILON)
    step_count = levels_now.astype(jnp.float32)[:, None]
    offset = 0.25 + 0.25 * (rows_now[:, None] + columns_now[None, :])
    ratio = jnp.abs(gradient) / bucket_norm * step_count
    lower = jnp.floor(ratio)
    quantum = lower + jnp.clip(2.0 * (ratio - lower - offset) + 0.5, 0.0, 1.0)
    return jnp.sign(gradient) * bucket_norm * quantum / step_count


def on_device(
    tile_tokens,
    proj_weight,
    text_hidden,
    cotangent,
    norm_gain,
    placeholders,
    bucket_levels,
    row_draws,
    column_draws,
):
    seq_count = lax.axis_size("seq")
    seq_index = lax.axis_index("seq")
    replicas = lax.axis_size(DP)
    places = placeholders[0]
    image_total = places.shape[0]
    tok_rows = text_hidden.shape[1]
    model_width = text_hidden.shape[2]
    columns = proj_weight.shape[1]
    all_positions = tok_rows * seq_count
    zero_half = jnp.zeros((), jnp.bfloat16)
    own_text = text_hidden[0]
    own_cot = cotangent[0]
    gathered = lax.all_gather(tile_tokens[0], "seq", axis=0, tiled=True)
    patch_block = gathered
    embedded = jnp.dot(
        patch_block,
        lax.all_gather(proj_weight, DP, axis=0, tiled=True),
        preferred_element_type=jnp.float32,
    ).astype(jnp.bfloat16)
    image_marks = jnp.zeros((all_positions,), jnp.int32).at[places].set(1)
    local_marks = lax.dynamic_slice_in_dim(image_marks, seq_index * tok_rows, tok_rows)
    is_image = local_marks[:, None] == 1
    owners = places // tok_rows
    owner_ids = jnp.arange(seq_count, dtype=jnp.int32)
    counts = jnp.sum((owners[:, None] == owner_ids[None, :]).astype(jnp.int32), axis=0)
    starts = jnp.cumsum(counts) - counts
    own_start = starts[seq_index]
    own_count = counts[seq_index]
    slot_ids = jnp.arange(IMG_MOST, dtype=jnp.int32)
    source_rows = jnp.clip(own_start + slot_ids, 0, image_total - 1)
    local_slots = jnp.clip(jnp.take(places, source_rows) - seq_index * tok_rows, 0, tok_rows - 1)
    slot_live = (slot_ids < own_count)[:, None]
    flat_index = owners * IMG_MOST + (
        jnp.arange(image_total, dtype=jnp.int32) - jnp.take(starts, owners)
    )
    outgoing = jnp.where(slot_live, jnp.take(own_cot, local_slots, axis=0), zero_half)
    returned = lax.all_to_all(outgoing[None], "seq", split_axis=2, concat_axis=0, tiled=True)
    image_cot = jnp.take(returned.reshape(-1, columns), flat_index, axis=0).astype(jnp.float32)
    emb_float = embedded.astype(jnp.float32)
    column_gain = lax.dynamic_slice_in_dim(norm_gain, seq_index * columns, columns)
    grad_in = image_cot * column_gain[None, :]
    squares, mixed = in_one(
        (jnp.sum(emb_float * emb_float, axis=1), jnp.sum(grad_in * emb_float, axis=1)), "seq"
    )
    inverse = lax.rsqrt(squares / model_width + EPSILON)[:, None]
    normed = emb_float * inverse
    emb_grad = ((grad_in - normed * (mixed[:, None] * inverse / model_width)) * inverse).astype(
        jnp.bfloat16
    )
    image_part = jnp.sum(image_cot * normed, axis=0)
    text_float = own_text.astype(jnp.float32)
    text_inverse = lax.rsqrt(jnp.mean(text_float * text_float, axis=1, keepdims=True) + EPSILON)
    text_terms = own_cot.astype(jnp.float32) * text_float * text_inverse
    text_part = jnp.sum(jnp.where(is_image, 0.0, text_terms), axis=0)
    placed_part = lax.dynamic_update_slice_in_dim(
        jnp.zeros((model_width,), jnp.float32), image_part, seq_index * columns, 0
    )
    gain_part = text_part + placed_part
    own_levels = bucket_levels[0, 0]
    own_row_draws = row_draws[0, 0]
    own_column_draws = column_draws[0]
    patch_block = gathered
    gradient = lax.dot_general(
        patch_block, emb_grad, (((0,), (0,)), ((), ())), preferred_element_type=jnp.float32
    )
    summed = lax.psum_scatter(
        quantize(gradient, own_levels, own_row_draws, own_column_draws).astype(jnp.bfloat16),
        DP,
        scatter_dimension=0,
        tiled=True,
    ).astype(jnp.float32)
    gain_total = one_axis_at_a_time(gain_part, DP_SEQ)
    return (summed / replicas, gain_total / replicas)


def solution(mesh):
    finer = Mesh(mesh.devices.reshape(4, 4, 2, mesh.shape["seq"]), ("dp_0", "dp_1", "dp_2", "seq"))
    return jax.shard_map(
        on_device,
        mesh=finer,
        in_specs=(
            P(DP, "seq", None),
            P(DP, "seq"),
            P(DP, "seq", None),
            P(DP, "seq", None),
            P(),
            P(DP, None),
            P(DP, "seq", None),
            P(DP, "seq", None),
            P(DP, "seq"),
        ),
        out_specs=(P(DP, "seq"), P()),
        check_vma=False,
    )
```

profile of v0, /device:TPU:6, one launch (start us, length us, event | category | flops | bytes accessed | tf_op | source)
XLA Modules:
  0.0 358.7 jit_solution(13340607720197606231)
XLA Ops:
  7.2 0.0 all-gather.7.cloned.1.call-start
  7.2 0.7 all-gather.7.cloned.1.call-update
  7.9 0.0 all-gather.5.cloned.1.call-start
  7.9 0.7 all-gather.5.cloned.1.call-update
  8.6 0.7 add_select_fusion
  9.3 0.1 convert_reduce_fusion
  9.5 0.1 copy.36
  9.6 0.1 reduce.3
  9.7 0.6 dynamic_slice.12
  10.3 0.7 fusion.39
  11.1 0.7 fusion.37
  11.8 1.5 gather_fusion
  13.2 0.7 fusion.36
  13.9 3.6 %gather_fusion.1 = bf16[48,8192]{1,0:T(8,128)(2,1)S(1)} fusion(bf16[128,8192]{1,0:T(8,128)(2,1)} %bitcast.91, s32[1024]{0:T(1024)S(1)} %pad_clamp_fusion.1), kind=kCustom, calls=%fused_computation.1 | custom fusion | bytes 1573056 | tf_op jit(solution)/shard_map/jit(_take)/gather | solution.py:94
  17.6 1.3 compare_and_fusion
  18.9 0.2 fusion.25
  19.0 6.8 %copy.37 = bf16[1,48,8192]{1,0,2:T(2,128)(2,1)} copy(bf16[1,48,8192]{2,1,0:T(8,128)(2,1)S(1)} %fusion.25) | data formatting | bytes 1572864 | tf_op jit(solution)/shard_map/jit(_where)/select_n | solution.py:94
  25.9 0.5 broadcast.663
  26.4 45.1 %reduce.24 = bf16[8192,48]{1,0:T(8,128)(2,1)S(1)} reduce(bf16[8192,1,48]{2,1,0:T(2,128)(2,1)} %bitcast.93, bf16[]{:T(256)} %broadcast.663), dimensions={1}, to_apply=%bitcast.79.reduce_sub_computation | reduce | bytes 1572866
  71.5 3.9 %reshape.481 = bf16[16,2,12288]{2,1,0:T(2,128)(2,1)} reshape(bf16[8192,48]{1,0:T(8,128)(2,1)S(1)} %reduce.24) | data formatting | bytes 1572864
  75.4 15.2 %all-to-all-start = ((bf16[16,2,12288]{2,1,0:T(2,128)(2,1)}), bf16[16,2,12288]{2,1,0:T(2,128)(2,1)S(1)}, u32[]{:S(2)}, u32[]{:S(2)}) async-start(bf16[16,2,12288]{2,1,0:T(2,128)(2,1)} %reshape.481), calls=%async_computation | async-start | bytes 1572864 | tf_op jit(solution)/shard_map/all_to_all | solution.py:95
  90.6 0.8 dynamic_slice.14
  91.4 0.0 copy-done
  91.4 4.3 %compare_select_fusion.2 = (s32[512,1]{0,1:T(1,128)S(1)}, s32[512,1]{0,1:T(1,128)S(1)}, s32[512,1]{0,1:T(1,128)S(1)}, s32[512,1]{0,1:T(1,128)S(1)}) fusion(s32[]{:T(128)} %bitcast.12, s32[]{:T(128)} %bitcast.13, s32[]{:T(128)} %bitcast.14, s32[]{:T(128)} %bitcast.15, s32[]{:T(128)} %bitcast.16, s32[]{:T(128)} %bitcast.18, s32[]{:T(128)} %bitcast.17, ...), kind=kLoop, calls=%fused_computation.62 | loop fusion | flops 16384 | bytes 10268 | tf_op jit(solution)/shard_map/jit(_take)/gather | solution.py:92
  95.7 0.1 compare_reduce_fusion.8
  95.8 5.8 %compare_and_fusion.1 = (pred[512]{0:T(512)(128)(4,1)S(1)}, s32[512]{0:T(512)S(1)}) fusion(pred[512]{0:T(512)(128)(4,1)S(1)} %get-tuple-element.24, pred[512]{0:T(512)(128)(4,1)S(1)} %get-tuple-element.22, pred[512]{0:T(512)(128)(4,1)S(1)} %get-tuple-element.23, pred[512]{0:T(512)(128)(4,1)S(1)} %get-tuple-element.21, ...), kind=kLoop, calls=%fused_computation.102 | loop fusion | flops 20480 | bytes 11300 | tf_op jit(solution)/shard_map/jit(_take)/and | solution.py:96
  101.6 36.3 %all-to-all-done = bf16[16,2,12288]{2,1,0:T(2,128)(2,1)S(1)} async-done(((bf16[16,2,12288]{2,1,0:T(2,128)(2,1)}), bf16[16,2,12288]{2,1,0:T(2,128)(2,1)S(1)}, u32[]{:S(2)}, u32[]{:S(2)}) %all-to-all-start) | async-done | bytes 786464 | tf_op jit(solution)/shard_map/all_to_all | solution.py:95
  137.9 7.9 %reshape.482 = bf16[8192,1,48]{2,1,0:T(2,128)(2,1)} reshape(bf16[16,2,12288]{2,1,0:T(2,128)(2,1)S(1)} %all-to-all-done) | data formatting | bytes 1572864
  145.8 8.1 %copy.38 = bf16[1,48,8192]{2,1,0:T(8,128)(2,1)S(1)} copy(bf16[1,48,8192]{1,0,2:T(2,128)(2,1)} %bitcast.94) | data formatting | bytes 1572864 | tf_op jit(solution)/shard_map/all_to_all | solution.py:95
  154.0 0.2 copy.48
  154.2 0.1 bitcast_bitcast_fusion
  154.3 0.4 copy.39
  154.7 2.0 gather_fusion.2
  156.7 1.0 copy.40
  157.7 3.7 %reshape.455 = bf16[3200,512]{1,0:T(8,128)(2,1)S(1)} reshape(bf16[32,100,512]{2,1,0:T(8,128)(2,1)} %all-gather.7.cloned.1.call-done) | data formatting | bytes 6553600
  161.5 19.4 %all-gather.5.cloned.1.call-done = bf16[1,512,3200]{2,1,0:T(8,128)(2,1)} async-done(((bf16[1,32,3200]{2,1,0:T(8,128)(2,1)}), bf16[1,512,3200]{2,1,0:T(8,128)(2,1)}) %all-gather.5.cloned.1.call-update) | async-done | bytes 3276816 | tf_op jit(solution)/shard_map/all_gather | solution.py:71
  180.8 4.9 %fusion.23 = (f32[512]{0:T(512)S(1)}, f32[512]{0:T(512)S(1)}, bf16[512,512]{0,1:T(8,128)(2,1)}) fusion(f32[512]{0:T(512)S(1)} %dynamic_slice.14, bf16[512,512]{0,1:T(8,128)(2,1)} %copy.40, pred[512]{0:T(512)(128)(4,1)S(1)} %get-tuple-element.25, bf16[3200,512]{1,0:T(8,128)(2,1)S(1)} %reshape.455, bf16[1,512,3200]{2,1,0:T(8,128)(2,1)} %all-gather.5.cloned.1.call-done), kind=kOutput, calls=%fused_computation.35 | convolution fusion | flops 1680079872 | bytes 7608832 | tf_op jit(solution)/shard_map/dot_general | solution.py:73
  185.7 0.7 broadcast_in_dim.90
  186.4 6.6 %all-to-all-start.1 = ((f32[16,1,1024]{2,1,0:T(1,128)}), f32[16,1,1024]{2,1,0:T(1,128)S(1)}, u32[]{:S(2)}, u32[]{:S(2)}) async-start(f32[16,1,1024]{2,1,0:T(1,128)} %broadcast_in_dim.90), calls=%async_computation.1 | async-start | bytes 131072 | tf_op jit(solution)/shard_map/all_to_all | solution.py:15
  193.0 0.0 all-reduce.3.cloned.1.call-start
  193.1 2.7 scatter_custom_fusion
  195.8 0.0 copy-done.4
  195.8 10.0 %all-to-all-done.1 = f32[16,1,1024]{2,1,0:T(1,128)S(1)} async-done(((f32[16,1,1024]{2,1,0:T(1,128)}), f32[16,1,1024]{2,1,0:T(1,128)S(1)}, u32[]{:S(2)}, u32[]{:S(2)}) %all-to-all-start.1) | async-done | bytes 65568 | tf_op jit(solution)/shard_map/all_to_all | solution.py:15
  205.8 0.1 reduce_sum.77
  205.9 0.0 copy-start.6
  205.9 4.4 %multiply_reduce_fusion = (f32[3200]{0:T(1024)S(1)}, f32[512,3200]{1,0:T(8,128)S(1)}) fusion(bf16[1,512,3200]{2,1,0:T(8,128)(2,1)} %all-gather.5.cloned.1.call-done, bf16[512,512]{0,1:T(8,128)(2,1)} %get-tuple-element.50, f32[512]{0:T(512)S(1)} %get-tuple-element.31, f32[512]{0:T(512)S(1)} %get-tuple-element.30, f32[512]{0:T(512)S(1)} %dynamic_slice.14, ...), kind=kOutput, calls=%fused_computation.12 | convolution fusion | flops 1683354496 | bytes 10898432 | tf_op jit(solution)/shard_map/dot_general | solution.py:121
  210.3 0.0 copy-done.6
  210.3 6.5 %fusion.6 = bf16[3200,512]{0,1:T(8,128)(2,1)} fusion(f32[512,3200]{1,0:T(8,128)S(1)} %get-tuple-element.52, f32[3200]{0:T(1024)S(1)} %convert_reduce_fusion.1, f32[512]{0:T(512)S(1)} %bitcast.103, f32[3200]{0:T(1024)S(1)} %reduce.13, f32[3200]{0:T(1024)S(1)} %add_sqrt_fusion), kind=kLoop, calls=%fused_computation.13 | loop fusion | flops 29491200 | bytes 9870848 | tf_op jit(solution)/shard_map/convert_element_type | solution.py:125
  216.8 0.0 all-reduce.3.cloned.1.call-update
  216.8 0.1 dynamic-slice_compare_fusion
  216.9 1.4 dynamic-slice.1
  218.9 2.1 fusion.10
  221.0 0.0 copy-done.1
  221.0 2.5 fusion.9
  223.5 0.3 fusion.22
  223.8 0.2 add_dynamic-update-slice_fusion
  224.0 14.2 %psum.28 = f32[8192]{0:T(1024)S(1)} all-reduce(f32[8192]{0:T(1024)S(1)} %add_dynamic-update-slice_fusion), channel_id=1, replica_groups=mesh['dp_0'=4,'dp_1'=4,'dp_2'=2,'seq'=16] {'dp_0'}, use_global_device_ids=true, to_apply=%region_11.12 | all-reduce | flops 8192 | bytes 65536 | tf_op jit(solution)/shard_map/psum | solution.py:34
  238.2 17.1 %psum.29 = f32[8192]{0:T(1024)S(1)} all-reduce(f32[8192]{0:T(1024)S(1)} %psum.28), channel_id=1, replica_groups=mesh['dp_0'=4,'dp_1'=4,'dp_2'=2,'seq'=16] {'dp_1'}, use_global_device_ids=true, to_apply=%region_12.13 | all-reduce | flops 8192 | bytes 65536 | tf_op jit(solution)/shard_map/psum | solution.py:34
  255.3 3.4 psum.30
  258.7 54.0 %psum.31 = f32[8192]{0:T(1024)S(1)} all-reduce(f32[8192]{0:T(1024)S(1)} %psum.30), channel_id=1, replica_groups=mesh['dp_0'=4,'dp_1'=4,'dp_2'=2,'seq'=16] {'seq'}, use_global_device_ids=true, to_apply=%region_14.15 | all-reduce | flops 8192 | bytes 65536 | tf_op jit(solution)/shard_map/psum | solution.py:34
  312.7 0.6 broadcast_multiply_fusion
  313.3 37.0 %all-reduce.3.cloned.1.call-done = bf16[3200,512]{0,1:T(8,128)(2,1)} async-done(((bf16[3200,512]{0,1:T(8,128)(2,1)}), bf16[3200,512]{0,1:T(8,128)(2,1)}) %all-reduce.3.cloned.1.call-update) | async-done | bytes 3276816
  350.3 1.1 convert_multiply_fusion.7
  351.4 0.8 copy.42
  (23 shorter events, 0.2 us)
Async XLA Ops:
  7.2 150.5 %all-gather.7.cloned.1.call-start = ((), (), s32[]{:S(2)}) async-start(), calls=%async_computation.3 | async-start | bytes 3514368 | tf_op jit(solution)/shard_map/all_gather | solution.py:75
  7.9 172.9 %all-gather.5.cloned.1.call-start = ((), (), s32[]{:S(2)}) async-start(), calls=%async_computation.2 | async-start | bytes 3481600 | tf_op jit(solution)/shard_map/all_gather | solution.py:71
  26.4 65.0 %copy-start = (s32[1,512]{1,0:T(1,128)S(1)}, s32[1,512]{1,0:T(1,128)}, u32[]{:S(2)}) copy-start(s32[1,512]{1,0:T(1,128)} %param.14) | copy-start | bytes 6148
  75.4 62.5 %all-to-all-start = ((bf16[16,2,12288]{2,1,0:T(2,128)(2,1)}), bf16[16,2,12288]{2,1,0:T(2,128)(2,1)S(1)}, u32[]{:S(2)}, u32[]{:S(2)}) async-start(bf16[16,2,12288]{2,1,0:T(2,128)(2,1)} %reshape.481), calls=%async_computation | async-start | bytes 1572864 | tf_op jit(solution)/shard_map/all_to_all | solution.py:95
  180.8 12.2 %copy-start.5 = (f32[1,1,3200]{2,1,0:T(1,128)S(1)}, f32[1,1,3200]{2,1,0:T(1,128)}, u32[]{:S(2)}) copy-start(f32[1,1,3200]{2,1,0:T(1,128)} %param.16) | copy-start | bytes 38404
  180.8 14.9 %copy-start.4 = (s32[1,1,3200]{2,1,0:T(1,128)S(1)}, s32[1,1,3200]{2,1,0:T(1,128)}, u32[]{:S(2)}) copy-start(s32[1,1,3200]{2,1,0:T(1,128)} %param.15) | copy-start | bytes 38404
  186.4 19.4 %all-to-all-start.1 = ((f32[16,1,1024]{2,1,0:T(1,128)}), f32[16,1,1024]{2,1,0:T(1,128)S(1)}, u32[]{:S(2)}, u32[]{:S(2)}) async-start(f32[16,1,1024]{2,1,0:T(1,128)} %broadcast_in_dim.90), calls=%async_computation.1 | async-start | bytes 131072 | tf_op jit(solution)/shard_map/all_to_all | solution.py:15
  193.0 157.3 %all-reduce.3.cloned.1.call-start = ((), (), s32[]{:S(2)}) async-start(), calls=%async_computation.4 | async-start | bytes 6553600
  205.9 4.4 %copy-start.6 = (f32[1,512]{1,0:T(1,128)S(1)}, f32[1,512]{1,0:T(1,128)}, u32[]{:S(2)}) copy-start(f32[1,512]{1,0:T(1,128)} %param.17) | copy-start | bytes 6148
  216.8 4.3 %copy-start.1 = (bf16[1,128,8192]{2,1,0:T(8,128)(2,1)S(1)}, bf16[1,128,8192]{2,1,0:T(8,128)(2,1)}, u32[]{:S(2)}) copy-start(bf16[1,128,8192]{2,1,0:T(8,128)(2,1)} %param.12) | copy-start | bytes 6291460
  216.8 6.8 %copy-start.2 = (bf16[512,512]{0,1:T(8,128)(2,1)S(1)}, bf16[512,512]{0,1:T(8,128)(2,1)}, u32[]{:S(2)}) copy-start(bf16[512,512]{0,1:T(8,128)(2,1)} %copy.40) | copy-start | bytes 1572868
  216.8 6.8 %copy-start.3 = (bf16[512,512]{0,1:T(8,128)(2,1)S(1)}, bf16[512,512]{0,1:T(8,128)(2,1)}, u32[]{:S(2)}) copy-start(bf16[512,512]{0,1:T(8,128)(2,1)} %get-tuple-element.50) | copy-start | bytes 1572868
Sparse Core Ops, SparseCore 0:
  11.1 64.6 all-gather.6
  77.9 102.9 all-gather.4
  216.9 133.3 all-reduce.2
where the time goes:
time: 360 us; the launch traced here: 359 us
  waiting for transfers between devices  104 us (29%)
  blocking collectives  88.7 us (25%)
  other arithmetic  72.6 us (20%)
  local copies, waits for them, and re-layouts  47.6 us (13%)
  starting transfers between devices  21.9 us (6%)
  between operations  14.7 us (4%)
  matrix products  9.27 us (3%)
    psum x4, blocking collectives, one_axis_at_a_time(): value = lax.psum(value, axis)  88.7 us
    unnamed x2, other arithmetic  45.2 us
    unnamed x4, waiting for transfers between devices  38.4 us
    all_to_all x1, waiting for transfers between devices, on_device(): lax.all_to_all(outgoing[None], 'seq', split_axis=2, concat_axis=0, tiled=...  36.3 us
    all_gather x1, waiting for transfers between devices, on_device(): gathered = lax.all_gather(tile_tokens[0], 'seq', axis=0, tiled=True)  19.4 us
    unnamed x21, local copies, waits for them, and re-layouts  18.5 us
    all_to_all x1, starting transfers between devices, on_device(): lax.all_to_all(outgoing[None], 'seq', split_axis=2, concat_axis=0, tiled=...  15.2 us
    all_to_all x1, waiting for transfers between devices, copy_for_each(): return lax.all_to_all(copies, axis, split_axis=0, concat_axis=0, tiled=True)  9.99 us
  transfers between devices with their start and end apart: 5, of which 4 were waited for; matrix products, arithmetic and copies ran while one was open for 31% of the time, Pallas kernels for 0%

commit v1 on v0

--- a/solution.py
+++ b/solution.py
@@ -92,7 +92,12 @@
         jnp.arange(image_total, dtype=jnp.int32) - jnp.take(starts, owners)
     )
     outgoing = jnp.where(slot_live, jnp.take(own_cot, local_slots, axis=0), zero_half)
-    returned = lax.all_to_all(outgoing[None], "seq", split_axis=2, concat_axis=0, tiled=True)
+    returned = jnp.concatenate(
+        lax.all_to_all(
+            jnp.stack(jnp.split(outgoing[None], lax.axis_size("seq"), axis=2)), "seq", 0, 0
+        ),
+        axis=0,
+    )
     image_cot = jnp.take(returned.reshape(-1, columns), flat_index, axis=0).astype(jnp.float32)
     emb_float = embedded.astype(jnp.float32)
     column_gain = lax.dynamic_slice_in_dim(norm_gain, seq_index * columns, columns)

time: 360 us -> 334 us (0.928)
  other arithmetic: 72.6 us -> 27.5 us
  waiting for transfers between devices: 104 us -> 141 us
  local copies, waits for them, and re-layouts: 47.6 us -> 29.4 us
    unnamed x2 -> x1, other arithmetic: 45.2 us -> 0.04 us
    all_gather x1, waiting for transfers between devices: 19.4 us -> 64.1 us  [on_device(): gathered = lax.all_gather(tile_tokens[0], 'seq', axis=0, tiled=True)]
    all_to_all x3 -> x0, local copies, waits for them, and re-layouts: 8.62 us -> none  [on_device(): lax.all_to_all(outgoing[None], 'seq', split_axis=2, concat_axis=0, tiled=...]
    all_to_all x1, waiting for transfers between devices: 36.3 us -> 28.3 us  [on_device(): lax.all_to_all(jnp.stack(jnp.split(outgoing[None], lax.axis_size('seq'),...]
    select_n x1 -> x0, local copies, waits for them, and re-layouts: 6.83 us -> none  [on_device(): jnp.where(slot_live, jnp.take(own_cot, local_slots, axis=0), zero_half)]
    unnamed x21 -> x32, local copies, waits for them, and re-layouts: 18.5 us -> 15.2 us
  transfers between devices with their start and end apart: 5 -> 5, of which waited for: 4 -> 4; matrix products, arithmetic and copies ran while one was open for 31% -> 14% of each run, Pallas kernels for 0% -> 0%
where the time goes in v1:
time: 334 us; the launch traced here: 333 us
  waiting for transfers between devices  141 us (42%)
  blocking collectives  88.4 us (26%)
  local copies, waits for them, and re-layouts  29.4 us (9%)
  other arithmetic  27.5 us (8%)
  starting transfers between devices  22.8 us (7%)
  between operations  14.7 us (4%)
  matrix products  9.25 us (3%)
    psum x4, blocking collectives, one_axis_at_a_time(): value = lax.psum(value, axis)  88.4 us
    all_gather x1, waiting for transfers between devices, on_device(): gathered = lax.all_gather(tile_tokens[0], 'seq', axis=0, tiled=True)  64.1 us
    unnamed x4, waiting for transfers between devices  38.3 us
    all_to_all x1, waiting for transfers between devices, on_device(): lax.all_to_all(jnp.stack(jnp.split(outgoing[None], lax.axis_size('seq'),...  28.3 us
    unnamed x32, local copies, waits for them, and re-layouts  15.2 us
    all_to_all x1, starting transfers between devices, on_device(): lax.all_to_all(jnp.stack(jnp.split(outgoing[None], lax.axis_size('seq'),...  15.2 us
    all_to_all x1, waiting for transfers between devices, copy_for_each(): return lax.all_to_all(copies, axis, split_axis=0, concat_axis=0, tiled=True)  10 us
    all_to_all x1, starting transfers between devices, copy_for_each(): return lax.all_to_all(copies, axis, split_axis=0, concat_axis=0, tiled=True)  7.51 us
  transfers between devices with their start and end apart: 5, of which 4 were waited for; matrix products, arithmetic and copies ran while one was open for 14% of the time, Pallas kernels for 0%

profile of v1, /device:TPU:6, one launch (start us, length us, event | category | flops | bytes accessed | tf_op | source)
XLA Modules:
  0.0 332.8 jit_solution(15616528988813262759)
XLA Ops:
  7.2 0.7 all-gather.7.cloned.1.call-update
  7.9 0.0 all-gather.5.cloned.1.call-start
  8.0 0.7 all-gather.5.cloned.1.call-update
  8.7 0.7 add_select_fusion
  9.4 0.1 convert_reduce_fusion
  9.5 0.1 copy.23
  9.6 0.1 reduce.3
  9.7 0.6 dynamic_slice.12
  10.3 0.7 fusion.55
  11.1 0.7 fusion.53
  11.8 1.5 gather_fusion
  13.3 0.7 fusion.52
  14.0 1.3 compare_and_fusion
  15.3 3.6 %gather_fusion.1 = bf16[48,8192]{1,0:T(8,128)(2,1)S(1)} fusion(bf16[128,8192]{1,0:T(8,128)(2,1)} %bitcast.145, s32[1024]{0:T(1024)S(1)} %pad_clamp_fusion.1), kind=kCustom, calls=%fused_computation.1 | custom fusion | bytes 1573056 | tf_op jit(solution)/shard_map/jit(_take)/gather | solution.py:94
  18.9 0.2 fusion.25
  19.1 0.6 fusion.46
  19.7 0.6 fusion.45
  20.3 0.6 fusion.44
  21.0 0.6 fusion.43
  21.6 0.6 fusion.42
  22.2 0.6 fusion.41
  22.8 0.6 fusion.40
  23.5 0.6 fusion.39
  24.1 0.6 fusion.38
  24.7 0.6 fusion.37
  25.3 0.6 fusion.36
  25.9 0.6 fusion.35
  26.5 0.6 fusion.34
  27.1 0.6 fusion.33
  27.8 0.6 fusion.32
  28.4 0.6 fusion.31
  29.0 15.2 %all-to-all-start = ((bf16[16,1,48,512]{3,2,1,0:T(8,128)(2,1)}), bf16[16,1,48,512]{3,2,1,0:T(8,128)(2,1)S(1)}, u32[]{:S(2)}, u32[]{:S(2)}) async-start(bf16[16,1,48,512]{3,2,1,0:T(8,128)(2,1)} %fusion.31), calls=%async_computation | async-start | bytes 1572864 | tf_op jit(solution)/shard_map/all_to_all | solution.py:96
  44.2 0.8 dynamic_slice.14
  45.0 4.4 %compare_select_fusion.2 = (s32[512,1]{0,1:T(1,128)S(1)}, s32[512,1]{0,1:T(1,128)S(1)}, s32[512,1]{0,1:T(1,128)S(1)}, s32[512,1]{0,1:T(1,128)S(1)}) fusion(s32[]{:T(128)} %bitcast.12, s32[]{:T(128)} %bitcast.13, s32[]{:T(128)} %bitcast.14, s32[]{:T(128)} %bitcast.15, s32[]{:T(128)} %bitcast.16, s32[]{:T(128)} %bitcast.18, s32[]{:T(128)} %bitcast.17, ...), kind=kLoop, calls=%fused_computation.93 | loop fusion | flops 16384 | bytes 10268 | tf_op jit(solution)/shard_map/jit(_take)/gather | solution.py:92
  49.4 0.1 compare_reduce_fusion.8
  49.5 5.7 %compare_and_fusion.1 = (pred[512]{0:T(512)(128)(4,1)S(1)}, s32[512]{0:T(512)S(1)}) fusion(pred[512]{0:T(512)(128)(4,1)S(1)} %get-tuple-element.22, pred[512]{0:T(512)(128)(4,1)S(1)} %get-tuple-element.20, pred[512]{0:T(512)(128)(4,1)S(1)} %get-tuple-element.21, pred[512]{0:T(512)(128)(4,1)S(1)} %get-tuple-element.19, ...), kind=kLoop, calls=%fused_computation.133 | loop fusion | flops 20480 | bytes 11300 | tf_op jit(solution)/shard_map/jit(_take)/and | solution.py:101
  55.2 28.3 %all-to-all-done = bf16[16,1,48,512]{3,2,1,0:T(8,128)(2,1)S(1)} async-done(((bf16[16,1,48,512]{3,2,1,0:T(8,128)(2,1)}), bf16[16,1,48,512]{3,2,1,0:T(8,128)(2,1)S(1)}, u32[]{:S(2)}, u32[]{:S(2)}) %all-to-all-start) | async-done | bytes 786464 | tf_op jit(solution)/shard_map/all_to_all | solution.py:96
  83.5 2.0 gather_fusion.2
  85.5 1.0 copy.24
  86.5 3.7 %reshape.450 = bf16[3200,512]{1,0:T(8,128)(2,1)S(1)} reshape(bf16[32,100,512]{2,1,0:T(8,128)(2,1)} %all-gather.7.cloned.1.call-done) | data formatting | bytes 6553600
  90.3 64.1 %all-gather.5.cloned.1.call-done = bf16[1,512,3200]{2,1,0:T(8,128)(2,1)} async-done(((bf16[1,32,3200]{2,1,0:T(8,128)(2,1)}), bf16[1,512,3200]{2,1,0:T(8,128)(2,1)}) %all-gather.5.cloned.1.call-update) | async-done | bytes 3276816 | tf_op jit(solution)/shard_map/all_gather | solution.py:71
  154.4 4.9 %fusion.23 = (f32[512]{0:T(512)S(1)}, f32[512]{0:T(512)S(1)}, bf16[512,512]{0,1:T(8,128)(2,1)}) fusion(f32[512]{0:T(512)S(1)} %dynamic_slice.14, bf16[512,512]{0,1:T(8,128)(2,1)} %copy.24, pred[512]{0:T(512)(128)(4,1)S(1)} %get-tuple-element.23, bf16[3200,512]{1,0:T(8,128)(2,1)S(1)} %reshape.450, bf16[1,512,3200]{2,1,0:T(8,128)(2,1)} %all-gather.5.cloned.1.call-done), kind=kOutput, calls=%fused_computation.35 | convolution fusion | flops 1680079872 | bytes 7608832 | tf_op jit(solution)/shard_map/dot_general | solution.py:73
  159.3 0.7 broadcast_in_dim.90
  159.9 7.5 %all-to-all-start.1 = ((f32[16,1,1024]{2,1,0:T(1,128)}), f32[16,1,1024]{2,1,0:T(1,128)S(1)}, u32[]{:S(2)}, u32[]{:S(2)}) async-start(f32[16,1,1024]{2,1,0:T(1,128)} %broadcast_in_dim.90), calls=%async_computation.1 | async-start | bytes 131072 | tf_op jit(solution)/shard_map/all_to_all | solution.py:15
  167.4 0.0 all-reduce.3.cloned.1.call-start
  167.6 2.6 scatter_custom_fusion
  170.2 10.0 %all-to-all-done.1 = f32[16,1,1024]{2,1,0:T(1,128)S(1)} async-done(((f32[16,1,1024]{2,1,0:T(1,128)}), f32[16,1,1024]{2,1,0:T(1,128)S(1)}, u32[]{:S(2)}, u32[]{:S(2)}) %all-to-all-start.1) | async-done | bytes 65568 | tf_op jit(solution)/shard_map/all_to_all | solution.py:15
  180.3 0.1 reduce_sum.77
  180.3 4.4 %multiply_reduce_fusion = (f32[3200]{0:T(1024)S(1)}, f32[512,3200]{1,0:T(8,128)S(1)}) fusion(bf16[1,512,3200]{2,1,0:T(8,128)(2,1)} %all-gather.5.cloned.1.call-done, bf16[512,512]{0,1:T(8,128)(2,1)} %get-tuple-element.48, f32[512]{0:T(512)S(1)} %get-tuple-element.29, f32[512]{0:T(512)S(1)} %get-tuple-element.28, f32[512]{0:T(512)S(1)} %dynamic_slice.14, ...), kind=kOutput, calls=%fused_computation.12 | convolution fusion | flops 1683354496 | bytes 10898432 | tf_op jit(solution)/shard_map/dot_general | solution.py:126
  184.8 6.4 %fusion.6 = bf16[3200,512]{0,1:T(8,128)(2,1)} fusion(f32[512,3200]{1,0:T(8,128)S(1)} %get-tuple-element.50, f32[3200]{0:T(1024)S(1)} %convert_reduce_fusion.1, f32[512]{0:T(512)S(1)} %bitcast.153, f32[3200]{0:T(1024)S(1)} %reduce.13, f32[3200]{0:T(1024)S(1)} %add_sqrt_fusion), kind=kLoop, calls=%fused_computation.13 | loop fusion | flops 29491200 | bytes 9870848 | tf_op jit(solution)/shard_map/convert_element_type | solution.py:130
  191.2 0.1 dynamic-slice_compare_fusion
  191.3 1.3 dynamic-slice.1
  193.3 2.1 fusion.10
  195.4 2.5 fusion.9
  197.9 0.3 fusion.22
  198.2 0.2 add_dynamic-update-slice_fusion
  198.4 14.1 %psum.28 = f32[8192]{0:T(1024)S(1)} all-reduce(f32[8192]{0:T(1024)S(1)} %add_dynamic-update-slice_fusion), channel_id=1, replica_groups=mesh['dp_0'=4,'dp_1'=4,'dp_2'=2,'seq'=16] {'dp_0'}, use_global_device_ids=true, to_apply=%region_11.12 | all-reduce | flops 8192 | bytes 65536 | tf_op jit(solution)/shard_map/psum | solution.py:34
  212.4 17.1 %psum.29 = f32[8192]{0:T(1024)S(1)} all-reduce(f32[8192]{0:T(1024)S(1)} %psum.28), channel_id=1, replica_groups=mesh['dp_0'=4,'dp_1'=4,'dp_2'=2,'seq'=16] {'dp_1'}, use_global_device_ids=true, to_apply=%region_12.13 | all-reduce | flops 8192 | bytes 65536 | tf_op jit(solution)/shard_map/psum | solution.py:34
  229.5 3.4 %psum.30 = f32[8192]{0:T(1024)S(1)} all-reduce(f32[8192]{0:T(1024)S(1)} %psum.29), channel_id=1, replica_groups=mesh['dp_0'=4,'dp_1'=4,'dp_2'=2,'seq'=16] {'dp_2'}, use_global_device_ids=true, to_apply=%region_13.14 | all-reduce | flops 8192 | bytes 65536 | tf_op jit(solution)/shard_map/psum | solution.py:34
  232.9 53.9 %psum.31 = f32[8192]{0:T(1024)S(1)} all-reduce(f32[8192]{0:T(1024)S(1)} %psum.30), channel_id=1, replica_groups=mesh['dp_0'=4,'dp_1'=4,'dp_2'=2,'seq'=16] {'seq'}, use_global_device_ids=true, to_apply=%region_14.15 | all-reduce | flops 8192 | bytes 65536 | tf_op jit(solution)/shard_map/psum | solution.py:34
  286.8 0.6 broadcast_multiply_fusion
  287.4 37.0 %all-reduce.3.cloned.1.call-done = bf16[3200,512]{0,1:T(8,128)(2,1)} async-done(((bf16[3200,512]{0,1:T(8,128)(2,1)}), bf16[3200,512]{0,1:T(8,128)(2,1)}) %all-reduce.3.cloned.1.call-update) | async-done | bytes 3276816
  324.4 1.1 convert_multiply_fusion.7
  325.4 0.8 copy.26
  (30 shorter events, 0.3 us)
Async XLA Ops:
  7.2 37.8 %copy-start = (s32[1,512]{1,0:T(1,128)S(1)}, s32[1,512]{1,0:T(1,128)}, u32[]{:S(2)}) copy-start(s32[1,512]{1,0:T(1,128)} %param.14) | copy-start | bytes 6148
  7.2 79.3 %all-gather.7.cloned.1.call-start = ((), (), s32[]{:S(2)}) async-start(), calls=%async_computation.3 | async-start | bytes 3514368 | tf_op jit(solution)/shard_map/all_gather | solution.py:75
  7.9 146.5 %all-gather.5.cloned.1.call-start = ((), (), s32[]{:S(2)}) async-start(), calls=%async_computation.2 | async-start | bytes 3481600 | tf_op jit(solution)/shard_map/all_gather | solution.py:71
  29.0 54.5 %all-to-all-start = ((bf16[16,1,48,512]{3,2,1,0:T(8,128)(2,1)}), bf16[16,1,48,512]{3,2,1,0:T(8,128)(2,1)S(1)}, u32[]{:S(2)}, u32[]{:S(2)}) async-start(bf16[16,1,48,512]{3,2,1,0:T(8,128)(2,1)} %fusion.31), calls=%async_computation | async-start | bytes 1572864 | tf_op jit(solution)/shard_map/all_to_all | solution.py:96
  90.2 77.2 %copy-start.5 = (f32[1,1,3200]{2,1,0:T(1,128)S(1)}, f32[1,1,3200]{2,1,0:T(1,128)}, u32[]{:S(2)}) copy-start(f32[1,1,3200]{2,1,0:T(1,128)} %param.16) | copy-start | bytes 38404
  90.3 79.9 %copy-start.4 = (s32[1,1,3200]{2,1,0:T(1,128)S(1)}, s32[1,1,3200]{2,1,0:T(1,128)}, u32[]{:S(2)}) copy-start(s32[1,1,3200]{2,1,0:T(1,128)} %param.15) | copy-start | bytes 38404
  159.2 25.5 %copy-start.6 = (f32[1,512]{1,0:T(1,128)S(1)}, f32[1,512]{1,0:T(1,128)}, u32[]{:S(2)}) copy-start(f32[1,512]{1,0:T(1,128)} %param.17) | copy-start | bytes 6148
  159.9 20.3 %all-to-all-start.1 = ((f32[16,1,1024]{2,1,0:T(1,128)}), f32[16,1,1024]{2,1,0:T(1,128)S(1)}, u32[]{:S(2)}, u32[]{:S(2)}) async-start(f32[16,1,1024]{2,1,0:T(1,128)} %broadcast_in_dim.90), calls=%async_computation.1 | async-start | bytes 131072 | tf_op jit(solution)/shard_map/all_to_all | solution.py:15
  167.4 156.9 %all-reduce.3.cloned.1.call-start = ((), (), s32[]{:S(2)}) async-start(), calls=%async_computation.4 | async-start | bytes 6553600
  184.8 10.6 %copy-start.1 = (bf16[1,128,8192]{2,1,0:T(8,128)(2,1)S(1)}, bf16[1,128,8192]{2,1,0:T(8,128)(2,1)}, u32[]{:S(2)}) copy-start(bf16[1,128,8192]{2,1,0:T(8,128)(2,1)} %param.12) | copy-start | bytes 6291460
  191.2 6.7 %copy-start.2 = (bf16[512,512]{0,1:T(8,128)(2,1)S(1)}, bf16[512,512]{0,1:T(8,128)(2,1)}, u32[]{:S(2)}) copy-start(bf16[512,512]{0,1:T(8,128)(2,1)} %copy.24) | copy-start | bytes 1572868
  191.2 6.7 %copy-start.3 = (bf16[512,512]{0,1:T(8,128)(2,1)S(1)}, bf16[512,512]{0,1:T(8,128)(2,1)}, u32[]{:S(2)}) copy-start(bf16[512,512]{0,1:T(8,128)(2,1)} %get-tuple-element.48) | copy-start | bytes 1572868
Sparse Core Ops, SparseCore 0:
  11.1 64.6 all-gather.6
  77.9 76.4 all-gather.4
  191.4 132.9 all-reduce.2
